TPU v7x, 32 devices: a whole 2x2x4 slice. The times are simulated.
32 devices in a mesh: pipe: 2 (over core), dp: 4 (over y, x), tensor: 4 (over z).
Axes of the slice: x: 2, y: 2, z: 4, core: 2. Of those that a mesh axis runs over, the one named last changes fastest.
Arguments:
- weights: bfloat16 [2, 8192, 8192], P('pipe', 'tensor', 'dp'), may hold values from -0.0625 to 0.0625
- inputs: bfloat16 [2, 2, 8, 64, 8192], P('pipe', None, 'dp', None, 'tensor'), may hold values from -150 to 150
- cotangent: bfloat16 [2, 8, 64, 8192], P(None, 'dp', None, 'tensor'), may hold values from -6 to 6
- clip_norm: float32 [1], replicated, may hold values from 8192 to 12582912
- noise: bfloat16 [2, 8192, 8192], P('pipe', 'tensor', 'dp'), may hold values from -6 to 6
Outputs:
- grads: float32 [2, 8192, 8192], P('pipe', 'tensor', 'dp')
- clip_factors: float32 [2, 8], P(None, 'dp')
All inputs are finite; a program needn't handle non-finite values.
Results may differ from a plain program's by a relative error of at most 0.015.
Values may be sent and summed in bfloat16 or wider, within the bound.
A program may use at most 128 MiB of HBM per device.

v0:
```python
import jax
import jax.numpy as jnp
from jax import lax
from jax.sharding import PartitionSpec as P


def shifted(value, axis, steps):
    count = lax.axis_size(axis)
    first, last = (max(0, -steps), min(count, count - steps))
    return lax.ppermute(value, axis, [(source, source + steps) for source in range(first, last)])


def local(weights, inputs, cotangent, clip_norm, noise):
    section_count = lax.axis_size("pipe")
    section_index = lax.axis_index("pipe")
    group_count = lax.axis_size("dp")
    weight_block = weights[0]
    local_inputs = inputs[0]
    micro_count, example_count, length_count, width_part = local_inputs.shape
    token_count = example_count * length_count
    column_part = weight_block.shape[1]
    full_width = column_part * group_count
    partial_grams = jnp.einsum(
        "mbld,mbkd->mblk", local_inputs, local_inputs, preferred_element_type=jnp.float32
    )
    input_grams = lax.psum(partial_grams.astype(jnp.bfloat16), "tensor").astype(jnp.float32)
    received = jnp.zeros((example_count, length_count, width_part), jnp.bfloat16)
    norm_part = jnp.zeros((micro_count, example_count), jnp.float32)
    stored = jnp.zeros((micro_count, group_count * token_count, column_part), jnp.bfloat16)
    micro_ids = jnp.arange(micro_count)
    for step_number in range(micro_count + section_count - 1):
        position = step_number - (section_count - 1 - section_index)
        is_running = jnp.logical_and(position >= 0, position < micro_count)
        chosen = jnp.clip(position, 0, micro_count - 1)
        incoming = lax.dynamic_index_in_dim(cotangent, chosen, 0, keepdims=False)
        current = jnp.where(section_index == section_count - 1, incoming, received)
        incoming_gradient = lax.all_gather(current, "tensor", axis=2, tiled=True)
        grad_grams = jnp.einsum(
            "xeh,xph->xep", incoming_gradient, incoming_gradient, preferred_element_type=jnp.float32
        )
        own_grams = lax.dynamic_index_in_dim(input_grams, chosen, 0, keepdims=False)
        section_terms = jnp.sum(grad_grams * own_grams, axis=(1, 2))
        picked = jnp.logical_and(is_running, micro_ids == chosen)
        norm_part = norm_part + jnp.where(picked[:, None], section_terms[None, :], 0.0)
        by_block = incoming_gradient.reshape(token_count, group_count, column_part)
        scattered_rows = lax.all_to_all(
            by_block, "dp", split_axis=1, concat_axis=0, tiled=True
        ).reshape(group_count * token_count, column_part)
        stored = jnp.where(
            is_running, lax.dynamic_update_index_in_dim(stored, scattered_rows, chosen, 0), stored
        )
        if step_number < micro_count + section_count - 2:
            summed = lax.psum_scatter(
                lax.dot_general(
                    scattered_rows,
                    weight_block,
                    (((1,), (1,)), ((), ())),
                    preferred_element_type=jnp.float32,
                ).astype(jnp.bfloat16),
                "dp",
                scatter_dimension=0,
                tiled=True,
            ).astype(jnp.float32)
            updated = current.reshape(token_count, width_part).astype(jnp.float32) + summed
            outgoing = updated.astype(jnp.bfloat16).reshape(example_count, length_count, width_part)
            received = shifted(outgoing, "pipe", -1)
    bound = clip_norm[0]
    totals = lax.psum(norm_part, "pipe")
    scale_terms = bound / jnp.maximum(jnp.sqrt(totals), bound)
    own_clipped = (local_inputs.astype(jnp.float32) * scale_terms[:, :, None, None]).astype(
        jnp.bfloat16
    )
    clipped = lax.all_gather(own_clipped, "dp", axis=1, tiled=True)
    flat_inputs = clipped.reshape(micro_count * group_count * token_count, width_part)
    flat_grads = stored.reshape(micro_count * group_count * token_count, column_part)
    summed_grad = lax.dot_general(
        flat_inputs, flat_grads, (((0,), (0,)), ((), ())), preferred_element_type=jnp.float32
    )
    noise_weight = 1.5 / full_width
    per_example_sum = micro_count * group_count * example_count
    final_output = (
        summed_grad + noise_weight * bound * noise[0].astype(jnp.float32)
    ) / per_example_sum
    return (final_output[None], scale_terms)


def solution(mesh):
    in_specs = (
        P("pipe", "tensor", "dp"),
        P("pipe", None, "dp", None, "tensor"),
        P(None, "dp", None, "tensor"),
        P(),
        P("pipe", "tensor", "dp"),
    )
    out_specs = (P("pipe", "tensor", "dp"), P(None, "dp"))
    return jax.shard_map(local, mesh=mesh, in_specs=in_specs, out_specs=out_specs, check_vma=False)
```

profile of v0, /device:TPU:0, one launch (start us, length us, event | category | flops | bytes accessed | tf_op | source)
XLA Modules:
  0.0 416.9 jit_solution(757374766356900355)
XLA Ops:
  9.2 49.1 %all-gather.12.cloned.1.call-done = bf16[1,2,64,8192]{3,2,1,0:T(8,128)(2,1)} async-done(((bf16[1,2,64,2048]{3,2,1,0:T(8,128)(2,1)}), bf16[1,2,64,8192]{3,2,1,0:T(8,128)(2,1)}) %all-gather.12.cloned.1.call-update) | async-done | bytes 2097168 | tf_op jit(solution)/shard_map/all_gather | solution.py:37
  58.2 3.3 reshape.85
  62.7 29.0 %all_to_all.45 = bf16[128,4,2048]{2,0,1:T(8,128)(2,1)S(1)} all-to-all(bf16[128,4,2048]{2,0,1:T(8,128)(2,1)S(1)} %copy.7), channel_id=1, replica_groups=mesh['pipe'=2,'dp'=4,'tensor'=4] {'dp'}, dimensions={1} | all-to-all | bytes 4194304 | tf_op jit(solution)/shard_map/all_to_all | solution.py:46
  93.1 5.8 %fusion.6 = bf16[512,2048]{1,0:T(8,128)(2,1)} fusion(bf16[512,2048]{1,0:T(8,128)(2,1)S(1)} %bitcast.82, bf16[1,2048,2048]{2,1,0:T(8,128)(2,1)S(1)} %copy-done.11), kind=kOutput, calls=%fused_computation.7 | convolution fusion | flops 4296015872 | bytes 12582912 | tf_op jit(solution)/shard_map/dot_general | solution.py:54
  98.9 32.8 %reduce-scatter.3.cloned.1.call-done = bf16[128,2048]{1,0:T(8,128)(2,1)} async-done(((bf16[512,2048]{1,0:T(8,128)(2,1)}), bf16[128,2048]{1,0:T(8,128)(2,1)}) %reduce-scatter.3.cloned.1.call-update) | async-done | bytes 524304 | tf_op jit(solution)/shard_map/reduce_scatter | solution.py:53
  134.3 2.5 collective-permute-done
  137.7 46.0 %all-gather.6.cloned.1.call-done = bf16[2,64,8192]{2,1,0:T(8,128)(2,1)} async-done(((bf16[2,64,2048]{2,1,0:T(8,128)(2,1)}), bf16[2,64,8192]{2,1,0:T(8,128)(2,1)}) %all-gather.6.cloned.1.call-update) | async-done | bytes 2097168 | tf_op jit(solution)/shard_map/all_gather | solution.py:37
  183.7 3.3 reshape.88
  188.2 28.8 %all_to_all.46 = bf16[128,4,2048]{2,0,1:T(8,128)(2,1)S(1)} all-to-all(bf16[128,4,2048]{2,0,1:T(8,128)(2,1)S(1)} %copy.8), channel_id=1, replica_groups=mesh['pipe'=2,'dp'=4,'tensor'=4] {'dp'}, dimensions={1} | all-to-all | bytes 4194304 | tf_op jit(solution)/shard_map/all_to_all | solution.py:46
  218.3 9.1 %fusion.9 = bf16[512,2048]{1,0:T(8,128)(2,1)} fusion(bf16[512,2048]{1,0:T(8,128)(2,1)S(1)} %bitcast.83, bf16[1,2048,2048]{2,1,0:T(8,128)(2,1)} %param.5), kind=kOutput, calls=%fused_computation.8 | convolution fusion | flops 4296015872 | bytes 12582912 | tf_op jit(solution)/shard_map/dot_general | solution.py:54
  227.5 32.9 %reduce-scatter.5.cloned.1.call-done = bf16[128,2048]{1,0:T(8,128)(2,1)} async-done(((bf16[512,2048]{1,0:T(8,128)(2,1)}), bf16[128,2048]{1,0:T(8,128)(2,1)}) %reduce-scatter.5.cloned.1.call-update) | async-done | bytes 524304 | tf_op jit(solution)/shard_map/reduce_scatter | solution.py:53
  268.4 20.9 %psum.14 = bf16[2,2,64,64]{3,2,1,0:T(8,128)(2,1)S(1)} all-reduce(bf16[2,2,64,64]{3,2,1,0:T(8,128)(2,1)S(1)} %convolution_convert_fusion), channel_id=1, replica_groups=mesh['pipe'=2,'dp'=4,'tensor'=4] {'tensor'}, use_global_device_ids=true, to_apply=%region_0.0 | all-reduce | flops 16384 | bytes 65536 | tf_op jit(solution)/shard_map/psum | solution.py:26
  289.4 3.0 fusion.19
  293.2 20.6 %all-gather.8.cloned.1.call-done = bf16[2,64,8192]{2,1,0:T(8,128)(2,1)} async-done(((bf16[2,64,2048]{2,1,0:T(8,128)(2,1)}), bf16[2,64,8192]{2,1,0:T(8,128)(2,1)}) %all-gather.8.cloned.1.call-update) | async-done | bytes 2097168 | tf_op jit(solution)/shard_map/all_gather | solution.py:37
  313.8 3.0 fusion.18
  317.7 2.7 psum.15
  321.7 2.8 reshape.92
  324.5 4.1 copy.9
  328.5 4.7 %all-to-all-start.2 = ((bf16[128,4,2048]{2,0,1:T(8,128)(2,1)}), bf16[128,4,2048]{2,0,1:T(8,128)(2,1)}, u32[]{:S(2)}, u32[]{:S(2)}) async-start(bf16[128,4,2048]{2,0,1:T(8,128)(2,1)} %copy.9), calls=%async_computation.4 | async-start | bytes 4194304 | tf_op jit(solution)/shard_map/all_to_all | solution.py:46
  338.2 3.8 constant_dynamic-update-slice_fusion.1
  342.1 23.3 %all-to-all-done.2 = bf16[128,4,2048]{2,0,1:T(8,128)(2,1)} async-done(((bf16[128,4,2048]{2,0,1:T(8,128)(2,1)}), bf16[128,4,2048]{2,0,1:T(8,128)(2,1)}, u32[]{:S(2)}, u32[]{:S(2)}) %all-to-all-start.2) | async-done | bytes 2097184 | tf_op jit(solution)/shard_map/all_to_all | solution.py:46
  365.4 4.5 %constant_dynamic-update-slice_fusion = bf16[2,512,2048]{2,1,0:T(8,128)(2,1)} fusion(bf16[2,512,2048]{2,1,0:T(8,128)(2,1)} %constant_dynamic-update-slice_fusion.1, s32[]{:T(128)S(6)} %min.12, bf16[128,4,2048]{2,0,1:T(8,128)(2,1)} %all-to-all-done.2, pred[]{:T(512)S(6)} %and.46), kind=kLoop, calls=%fused_computation.30 | loop fusion | flops 1048576 | bytes 6291461 | tf_op jit(solution)/shard_map/jit(_where)/select_n | solution.py:49
  369.9 22.9 %all-gather.10.cloned.1.call-done = bf16[2,8,64,2048]{3,2,1,0:T(8,128)(2,1)} async-done(((bf16[2,2,64,2048]{3,2,1,0:T(8,128)(2,1)}), bf16[2,8,64,2048]{3,2,1,0:T(8,128)(2,1)}) %all-gather.10.cloned.1.call-update) | async-done | bytes 4194320 | tf_op jit(solution)/shard_map/all_gather | solution.py:73
  392.8 17.3 %fusion.1 = f32[1,2048,2048]{2,1,0:T(8,128)} fusion(bf16[1,2048,2048]{2,1,0:T(8,128)(2,1)} %param.9, f32[]{:T(128)S(6)} %mul_shard_map.3, bf16[1024,2048]{1,0:T(8,128)(2,1)} %bitcast.87, bf16[1024,2048]{1,0:T(8,128)(2,1)} %bitcast.27), kind=kOutput, calls=%fused_computation.2 | convolution fusion | flops 8606711808 | bytes 33554436 | tf_op jit(solution)/shard_map/dot_general | solution.py:76
  (57 shorter events, 25.7 us)
Async XLA Ops:
  7.2 51.1 %all-gather.12.cloned.1.call-start = ((), (), s32[]{:S(2)}) async-start(), calls=%async_computation.10 | async-start | bytes 2621440 | tf_op jit(solution)/shard_map/all_gather | solution.py:37
  9.1 122.7 %reduce-scatter.3.cloned.1.call-start = ((), (), s32[]{:S(2)}) async-start(), calls=%async_computation.5 | async-start | bytes 2621440 | tf_op jit(solution)/shard_map/reduce_scatter | solution.py:53
  61.6 31.5 %copy-start.11 = (bf16[1,2048,2048]{2,1,0:T(8,128)(2,1)S(1)}, bf16[1,2048,2048]{2,1,0:T(8,128)(2,1)}, u32[]{:S(2)}) copy-start(bf16[1,2048,2048]{2,1,0:T(8,128)(2,1)} %param.5) | copy-start | bytes 25165828
  91.8 1.3 copy-start.2
  98.9 32.9 %copy-start.6 = (bf16[1,2,64,2048]{3,2,1,0:T(8,128)(2,1)S(1)}, bf16[1,2,64,2048]{3,2,1,0:T(8,128)(2,1)}, u32[]{:S(2)}) copy-start(bf16[1,2,64,2048]{3,2,1,0:T(8,128)(2,1)} %dynamic-slice_select_fusion) | copy-start | bytes 1572868
  98.9 37.9 %copy-start.8 = (bf16[2,2,64,2048]{3,2,1,0:T(8,128)(2,1)S(1)}, bf16[2,2,64,2048]{3,2,1,0:T(8,128)(2,1)}, u32[]{:S(2)}) copy-start(bf16[2,2,64,2048]{3,2,1,0:T(8,128)(2,1)} %param.7) | copy-start | bytes 3145732
  98.9 84.8 %all-gather.6.cloned.1.call-start = ((), (), s32[]{:S(2)}) async-start(), calls=%async_computation.6 | async-start | bytes 2621440 | tf_op jit(solution)/shard_map/all_gather | solution.py:37
  133.0 3.8 collective-permute-start
  137.6 122.7 %reduce-scatter.5.cloned.1.call-start = ((), (), s32[]{:S(2)}) async-start(), calls=%async_computation.7 | async-start | bytes 2621440 | tf_op jit(solution)/shard_map/reduce_scatter | solution.py:53
  217.0 1.4 copy-start.4
  227.4 32.9 %copy-start.7 = (bf16[2,64,2048]{2,1,0:T(8,128)(2,1)S(1)}, bf16[2,64,2048]{2,1,0:T(8,128)(2,1)}, u32[]{:S(2)}) copy-start(bf16[2,64,2048]{2,1,0:T(8,128)(2,1)} %bitcast_select_fusion.4) | copy-start | bytes 1572868
  227.5 86.4 %all-gather.8.cloned.1.call-start = ((), (), s32[]{:S(2)}) async-start(), calls=%async_computation.8 | async-start | bytes 2621440 | tf_op jit(solution)/shard_map/all_gather | solution.py:37
  261.6 3.8 collective-permute-start.1
  266.2 126.6 %all-gather.10.cloned.1.call-start = ((), (), s32[]{:S(2)}) async-start(), calls=%async_computation.9 | async-start | bytes 5242880 | tf_op jit(solution)/shard_map/all_gather | solution.py:73
  266.3 26.1 %copy-start = (bf16[2,64,8192]{2,1,0:T(8,128)(2,1)S(1)}, bf16[2,64,8192]{2,1,0:T(8,128)(2,1)}, u32[]{:S(2)}) copy-start(bf16[2,64,8192]{2,1,0:T(8,128)(2,1)} %all-gather.6.cloned.1.call-done) | copy-start | bytes 6291460
  293.2 27.2 %copy-start.9 = (bf16[1,2,2,64,2048]{4,3,2,1,0:T(8,128)(2,1)S(1)}, bf16[1,2,2,64,2048]{4,3,2,1,0:T(8,128)(2,1)}, u32[]{:S(2)}) copy-start(bf16[1,2,2,64,2048]{4,3,2,1,0:T(8,128)(2,1)} %param.6) | copy-start | bytes 3145732
  316.9 4.8 %copy-start.1 = (bf16[2,64,8192]{2,1,0:T(8,128)(2,1)S(1)}, bf16[2,64,8192]{2,1,0:T(8,128)(2,1)}, u32[]{:S(2)}) copy-start(bf16[2,64,8192]{2,1,0:T(8,128)(2,1)} %all-gather.8.cloned.1.call-done) | copy-start | bytes 6291460
  320.4 4.1 copy-start.10
  328.5 4.7 %copy-start.3 = (bf16[128,4,2048]{2,0,1:T(8,128)(2,1)S(1)}, bf16[128,4,2048]{2,0,1:T(8,128)(2,1)}, u32[]{:S(2)}) copy-start(bf16[128,4,2048]{2,0,1:T(8,128)(2,1)} %copy-done.2) | copy-start | bytes 6291460
  328.5 36.9 %all-to-all-start.2 = ((bf16[128,4,2048]{2,0,1:T(8,128)(2,1)}), bf16[128,4,2048]{2,0,1:T(8,128)(2,1)}, u32[]{:S(2)}, u32[]{:S(2)}) async-start(bf16[128,4,2048]{2,0,1:T(8,128)(2,1)} %copy.9), calls=%async_computation.4 | async-start | bytes 4194304 | tf_op jit(solution)/shard_map/all_to_all | solution.py:46
  335.9 2.3 copy-start.5
Sparse Core Ops, SparseCore 0:
  9.6 48.6 all-gather.11
  99.0 32.7 reduce-scatter.2
  137.8 45.9 all-gather.5
  227.6 32.7 reduce-scatter.4
  266.4 47.4 all-gather.7
  321.8 70.9 all-gather.9
where the time goes:
time: 418 us; the launch traced here: 417 us
  waiting for transfers between devices  233 us (56%)
  blocking collectives  81.4 us (19%)
  matrix products  41 us (10%)
  local copies, waits for them, and re-layouts  23.4 us (6%)
  other arithmetic  15.8 us (4%)
  between operations  15.1 us (4%)
  starting transfers between devices  7.54 us (2%)
    all_gather x3, waiting for transfers between devices, local(): incoming_gradient = lax.all_gather(current, 'tensor', axis=2, tiled=True)  116 us
    reduce_scatter x2, waiting for transfers between devices, local(): lax.psum_scatter(lax.dot_general(scattered_rows, weight_block, (((1,), (1...  65.7 us
    all_to_all x2, blocking collectives, local(): lax.all_to_all(by_block, 'dp', split_axis=1, concat_axis=0, tiled=True)  57.8 us
    all_to_all x1, waiting for transfers between devices, local(): lax.all_to_all(by_block, 'dp', split_axis=1, concat_axis=0, tiled=True)  23.3 us
    all_gather x1, waiting for transfers between devices, local(): clipped = lax.all_gather(own_clipped, 'dp', axis=1, tiled=True)  22.9 us
    psum x1, blocking collectives, local(): lax.psum(partial_grams.astype(jnp.bfloat16), 'tensor').astype(jnp.float32)  20.9 us
    dot_general x1, matrix products, local(): lax.dot_general(flat_inputs, flat_grads, (((0,), (0,)), ((), ())), prefer...  17.3 us
    reshape x6, local copies, waits for them, and re-layouts, local(): by_block = incoming_gradient.reshape(token_count, group_count, column_part)  15.8 us
  transfers between devices with their start and end apart: 9, of which 9 were waited for; matrix products, arithmetic and copies ran while one was open for 6% of the time, Pallas kernels for 0%

commit v1 on v0

--- a/solution.py
+++ b/solution.py
@@ -1,6 +1,8 @@
 import jax
 import jax.numpy as jnp
 from jax import lax
+from jax.experimental import pallas as pl
+from jax.experimental.pallas import tpu as pltpu
 from jax.sharding import PartitionSpec as P
 
 
@@ -84,6 +86,411 @@
     return (final_output[None], scale_terms)
 
 
+MESH = pl.DeviceIdType.MESH
+CHUNKS = 4
+
+
+def exchange_kernel(
+    bound_ref, w_hbm, x_ref, cot_ref,
+    xs_ref, factor_ref, g_ref,
+    w_ref, xg, zb1, zb2, g1c, bt, rs, gin_send, gin, nz, fb,
+    w_sem, w_recv, x_sem, x_recv, loc_sem, zs, zr, as1, ar1, as2, ar2,
+    rs_send, rs_recv, gs, gr, ns, nr, fs, fr, pair_send, pair_recv,
+):
+    p, d, t = lax.axis_index("pipe"), lax.axis_index("dp"), lax.axis_index("tensor")
+    sibling = 1 - p
+    xn = d + 1 - 2 * lax.rem(d, 2)
+    yn = lax.rem(d + 2, 4)
+    diagonal = 3 - d
+    chunk_rows, width = cot_ref.shape[2], cot_ref.shape[3]
+    tokens = CHUNKS * chunk_rows
+    half = tokens // 2
+
+    def remote(source, target, send, recv, place):
+        return pltpu.make_async_remote_copy(
+            src_ref=source, dst_ref=target, send_sem=send, recv_sem=recv,
+            device_id=place, device_id_type=MESH,
+        )
+
+    barrier = pltpu.get_barrier_semaphore()
+    places = [(sibling, d, t)]
+    for core in (p, sibling):
+        for step in range(1, 4):
+            places.append((core, d, lax.rem(t + step, 4)))
+            places.append((core, lax.rem(d + step, 4), t))
+    for place in places:
+        pl.semaphore_signal(barrier, inc=1, device_id=place, device_id_type=MESH)
+    pl.semaphore_wait(barrier, len(places))
+
+    def z_send(buf, phase, c, s, way):
+        place = (p, d, lax.rem(t + (1 if way == 0 else 3), 4))
+        return remote(buf.at[s, c], buf.at[s, c], zs.at[phase, c, s, way], zr.at[phase, c, s], place)
+
+    def own_send(buf, phase, c):
+        @pl.when(t < 3)
+        def _():
+            z_send(buf, phase, c, t, 0).start()
+
+        @pl.when(t > 0)
+        def _():
+            z_send(buf, phase, c, t, 1).start()
+
+    def spread_remote(phase, c, k):
+        if phase == 0:
+            return remote(zb1.at[k, c], g1c.at[d, c], as1.at[c, k], ar1.at[c, d], (p, k, t))
+        return remote(zb2.at[k, c], g_ref.at[p, d, c], as2.at[c, k], ar2.at[p, d, c], (0, k, t))
+
+    def spread_local(phase, c, k):
+        if phase == 0:
+            return pltpu.make_async_copy(zb1.at[k, c], g1c.at[d, c], ar1.at[c, d])
+        return pltpu.make_async_copy(zb2.at[k, c], g_ref.at[p, d, c], ar2.at[p, d, c])
+
+    def stays(phase, k):
+        return k == d if phase == 0 else jnp.logical_and(k == d, p == 0)
+
+    def spread(phase, c, k):
+        @pl.when(stays(phase, k))
+        def _():
+            spread_local(phase, c, k).start()
+
+        @pl.when(jnp.logical_not(stays(phase, k)))
+        def _():
+            spread_remote(phase, c, k).start()
+
+    def arrivals(buf, phase, c, distance):
+        low, high = t - distance, t + distance
+
+        @pl.when(low >= 0)
+        def _():
+            z_send(buf, phase, c, low, 0).wait_recv()
+
+            @pl.when(t < 3)
+            def _():
+                z_send(buf, phase, c, low, 0).start()
+
+            spread(phase, c, low)
+
+        @pl.when(high <= 3)
+        def _():
+            z_send(buf, phase, c, high, 1).wait_recv()
+
+            @pl.when(t > 0)
+            def _():
+                z_send(buf, phase, c, high, 1).start()
+
+            spread(phase, c, high)
+
+    own = [
+        pltpu.make_async_copy(cot_ref.at[p], zb1.at[t], loc_sem.at[0]),
+        pltpu.make_async_copy(x_ref, xg.at[d], loc_sem.at[1]),
+    ]
+    for copy in own:
+        copy.start()
+    own[0].wait()
+    own_send(zb1, 0, 0)
+    spread(0, 0, t)
+
+    w_local = pltpu.make_async_copy(w_hbm, w_ref, loc_sem.at[2])
+    w_remote = remote(w_hbm, w_ref, w_sem.at[0], w_recv.at[0], (sibling, d, t))
+
+    @pl.when(p == 1)
+    def _():
+        w_remote.start()
+        w_local.start()
+
+    x_sends = [
+        remote(x_ref, xg.at[d], x_sem.at[0], x_recv.at[0], (p, xn, t)),
+        remote(x_ref, xg.at[d], x_sem.at[1], x_recv.at[1], (p, yn, t)),
+    ]
+    for copy in x_sends:
+        copy.start()
+
+    def gram(block):
+        return lax.dot_general(
+            block, block, (((1,), (1,)), ((), ())), preferred_element_type=jnp.float32
+        )
+
+    for m in range(2):
+        gin_send[m] = gram(x_ref[m]).astype(jnp.bfloat16)
+    gram_sends = []
+    for core in range(2):
+        for step in range(4):
+            place = (lax.rem(p + core, 2), d, lax.rem(t + step, 4))
+            if core or step:
+                index = core * 4 + step
+                gram_sends.append(
+                    remote(gin_send.at[place[0]], gin.at[p, t], gs.at[index], gr.at[index], place)
+                )
+    for copy in gram_sends:
+        copy.start()
+    gin[p, t] = gin_send[p]
+
+    def first_round(c, carry):
+        arrivals(zb1, 0, c, 1)
+        arrivals(zb1, 0, c, 2)
+
+        @pl.when(c < CHUNKS - 1)
+        def _():
+            own_send(zb1, 0, c + 1)
+            spread(0, c + 1, t)
+
+        arrivals(zb1, 0, c, 3)
+
+        @pl.when(c == 0)
+        def _():
+            @pl.when(p == 1)
+            def _():
+                w_local.wait()
+
+            @pl.when(p == 0)
+            def _():
+                w_remote.wait_recv()
+
+        for j in range(4):
+            @pl.when(d == j)
+            def _():
+                spread_local(0, c, d).wait()
+
+            @pl.when(d != j)
+            def _():
+                remote(
+                    zb1.at[0, c], g1c.at[j, c], as1.at[c, 0], ar1.at[c, j], (p, lax.rem(d + 1, 4), t)
+                ).wait_recv()
+        rows = jnp.concatenate([g1c[j, c] for j in range(4)], axis=0)
+
+        def columns(n, inner):
+            start = pl.multiple_of(n * 256, 256)
+            terms = lax.dot_general(
+                rows, w_ref[pl.ds(start, 256), :], (((1,), (1,)), ((), ())),
+                preferred_element_type=jnp.float32,
+            ).astype(jnp.bfloat16)
+            for j in range(4):
+                bt[j, c, :, pl.ds(start, 256)] = terms[j * chunk_rows:(j + 1) * chunk_rows]
+            return inner
+
+        lax.fori_loop(0, width // 256, columns, 0)
+        for step in (3, 1, 2):
+            reduce_send(c, step).start()
+        return carry
+
+    def reduce_send(c, step):
+        target = lax.rem(d + step, 4)
+        return remote(
+            bt.at[target, c], rs.at[step - 1, c],
+            rs_send.at[c, step - 1], rs_recv.at[c, step - 1], (p, target, t),
+        )
+
+    lax.fori_loop(0, CHUNKS, first_round, 0)
+
+    pair_remote = remote(g1c, g_ref.at[0], pair_send.at[0], pair_recv.at[0], (sibling, d, t))
+    pair_local = pltpu.make_async_copy(g1c, g_ref.at[1], loc_sem.at[3])
+
+    @pl.when(p == 0)
+    def _():
+        pair_remote.start()
+
+    @pl.when(p == 1)
+    def _():
+        pair_local.start()
+
+    def make_own(c):
+        for step in range(1, 4):
+            reduce_send(c, step).wait_recv()
+        total = zb1[t, c].astype(jnp.float32)
+        part = bt[d, c].astype(jnp.float32)
+        for step in range(3):
+            part = part + rs[step, c].astype(jnp.float32)
+        zb2[t, c] = (total + part).astype(jnp.bfloat16)
+        own_send(zb2, 1, c)
+        spread(1, c, t)
+
+    remote(x_ref, xg.at[xn], x_sem.at[0], x_recv.at[0], (p, xn, t)).wait_recv()
+    remote(x_ref, xg.at[yn], x_sem.at[1], x_recv.at[1], (p, yn, t)).wait_recv()
+    forwards = [
+        remote(xg.at[xn, 0], xg.at[xn, 0], x_sem.at[2], x_recv.at[2], (p, yn, t)),
+        remote(xg.at[yn, 1], xg.at[yn, 1], x_sem.at[3], x_recv.at[3], (p, xn, t)),
+    ]
+    for copy in forwards:
+        copy.start()
+
+    make_own(0)
+
+    def second_round(c, carry):
+        arrivals(zb2, 1, c, 1)
+        make_own(c + 1)
+        arrivals(zb2, 1, c, 2)
+        arrivals(zb2, 1, c, 3)
+        return carry
+
+    lax.fori_loop(0, CHUNKS - 1, second_round, 0)
+
+    for copy in gram_sends:
+        copy.wait_recv()
+    sums = []
+    for section in range(2):
+        full = gin[section, 0].astype(jnp.float32)
+        for part in range(1, 4):
+            full = full + gin[section, part].astype(jnp.float32)
+        source = zb2 if section == 0 else zb1
+        sums.append(full * gram(jnp.concatenate([source[t, c] for c in range(CHUNKS)], axis=0)))
+    products = sums[0] + sums[1]
+    row = lax.broadcasted_iota(jnp.int32, (8, 128), 0)
+    nz[t] = jnp.where(
+        row == 0, jnp.sum(products[:half, :half]), jnp.sum(products[half:, half:])
+    )
+    norm_sends = [
+        remote(nz.at[t], nz.at[t], ns.at[step - 1], nr.at[step - 1], (p, d, lax.rem(t + step, 4)))
+        for step in range(1, 4)
+    ]
+    for copy in norm_sends:
+        copy.start()
+    arrivals(zb2, 1, CHUNKS - 1, 1)
+    for copy in norm_sends:
+        copy.wait_recv()
+    bound = bound_ref[0]
+    square = nz[0] + nz[1] + nz[2] + nz[3]
+    fb[p, d] = bound / jnp.maximum(jnp.sqrt(square), bound)
+    factor_sends = []
+    for core in range(2):
+        for step in range(4):
+            if core or step:
+                index = core * 4 + step
+                place = (lax.rem(p + core, 2), lax.rem(d + step, 4), t)
+                factor_sends.append(remote(fb.at[p, d], fb.at[p, d], fs.at[index], fr.at[index], place))
+    for copy in factor_sends:
+        copy.start()
+    arrivals(zb2, 1, CHUNKS - 1, 2)
+    arrivals(zb2, 1, CHUNKS - 1, 3)
+    for copy in factor_sends:
+        copy.wait_recv()
+    own[1].wait()
+    remote(xg.at[xn, 0], xg.at[diagonal, 0], x_sem.at[2], x_recv.at[2], (p, yn, t)).wait_recv()
+    remote(xg.at[yn, 1], xg.at[diagonal, 1], x_sem.at[3], x_recv.at[3], (p, xn, t)).wait_recv()
+
+    def scale(index, carry):
+        j, m = index // 2, lax.rem(index, 2)
+        tile = fb[m, j]
+        for e in range(2):
+            for piece in range(4):
+                spot = (pl.ds(e * half + piece * 16, 16), slice(None))
+                block = xg[(j, m) + spot].astype(jnp.float32)
+                xs_ref[(m, j) + spot] = (block * tile[e:e + 1, 0:1]).astype(jnp.bfloat16)
+        return carry
+
+    lax.fori_loop(0, 8, scale, 0)
+    for m in range(2):
+        factor_ref[m] = fb[m, d]
+
+    def finish(c, carry):
+        for phase, buf in ((0, zb1), (1, zb2)):
+            for s in range(4):
+                @pl.when(jnp.logical_and(s <= t, t < 3))
+                def _():
+                    z_send(buf, phase, c, s, 0).wait_send()
+
+                @pl.when(jnp.logical_and(s >= t, t > 0))
+                def _():
+                    z_send(buf, phase, c, s, 1).wait_send()
+
+                @pl.when(jnp.logical_not(stays(phase, s)))
+                def _():
+                    spread_remote(phase, c, s).wait_send()
+
+        for step in range(1, 4):
+            reduce_send(c, step).wait_send()
+
+        @pl.when(p == 0)
+        def _():
+            for m in range(2):
+                for j in range(4):
+                    here = jnp.logical_and(j == d, m == 0)
+
+                    @pl.when(here)
+                    def _():
+                        spread_local(1, c, d).wait()
+
+                    @pl.when(jnp.logical_not(here))
+                    def _():
+                        remote(
+                            zb2.at[0, c], g_ref.at[m, j, c], as2.at[c, 0], ar2.at[m, j, c], (1, d, t)
+                        ).wait_recv()
+        return carry
+
+    lax.fori_loop(0, CHUNKS, finish, 0)
+    for copy in x_sends + forwards + gram_sends + norm_sends + factor_sends:
+        copy.wait_send()
+
+    @pl.when(p == 0)
+    def _():
+        pair_remote.wait_send()
+
+    @pl.when(p == 1)
+    def _():
+        w_remote.wait_send()
+        pair_local.wait()
+        pair_remote.wait_recv()
+
+
+def fast_local(weights, inputs, cotangent, clip_norm, noise):
+    weight_block = weights[0]
+    width, column_part = weight_block.shape
+    micro_count, example_count, length_count, _ = inputs[0].shape
+    tokens = example_count * length_count
+    rows = tokens // CHUNKS
+    bf16, f32 = jnp.bfloat16, jnp.float32
+    x = inputs[0].reshape(micro_count, tokens, width)
+    cot = cotangent.reshape(micro_count, CHUNKS, rows, width)
+    vmem, dma = pltpu.VMEM, pltpu.SemaphoreType.DMA
+    shards = (4, CHUNKS, rows, width)
+    clipped, factors, gradients = pl.pallas_call(
+        exchange_kernel,
+        out_shape=(
+            jax.ShapeDtypeStruct((2, 4, tokens, width), bf16),
+            jax.ShapeDtypeStruct((2, 8, 128), f32),
+            jax.ShapeDtypeStruct((2,) + shards, bf16),
+        ),
+        in_specs=[
+            pl.BlockSpec(memory_space=pltpu.SMEM),
+            pl.BlockSpec(memory_space=pl.ANY),
+            pl.BlockSpec(memory_space=vmem),
+            pl.BlockSpec(memory_space=vmem),
+        ],
+        out_specs=(
+            pl.BlockSpec(memory_space=vmem),
+            pl.BlockSpec(memory_space=vmem),
+            pl.BlockSpec(memory_space=pl.ANY),
+        ),
+        scratch_shapes=[
+            vmem((width, column_part), bf16),
+            vmem((4, 2, tokens, width), bf16),
+            vmem(shards, bf16), vmem(shards, bf16), vmem(shards, bf16), vmem(shards, bf16),
+            vmem((3,) + shards[1:], bf16),
+            vmem((2, tokens, tokens), bf16),
+            vmem((2, 4, tokens, tokens), bf16),
+            vmem((4, 8, 128), f32),
+            vmem((2, 4, 8, 128), f32),
+            dma((1,)), dma((1,)), dma((4,)), dma((4,)), dma((4,)),
+            dma((2, CHUNKS, 4, 2)), dma((2, CHUNKS, 4)),
+            dma((CHUNKS, 4)), dma((CHUNKS, 4)), dma((CHUNKS, 4)), dma((2, 4, CHUNKS)),
+            dma((CHUNKS, 3)), dma((CHUNKS, 3)),
+            dma((8,)), dma((8,)), dma((3,)), dma((3,)), dma((8,)), dma((8,)),
+            dma((1,)), dma((1,)),
+        ],
+        compiler_params=pltpu.CompilerParams(
+            collective_id=0, has_side_effects=True, vmem_limit_bytes=50 * 1024 * 1024
+        ),
+        name="exchange",
+    )(clip_norm, weight_block, x, cot)
+    total = lax.dot_general(
+        clipped.reshape(-1, width), gradients.reshape(-1, column_part),
+        (((0,), (0,)), ((), ())), preferred_element_type=f32,
+    )
+    bound = clip_norm[0]
+    noise_weight = 1.5 / (column_part * 4)
+    final_output = (total + noise_weight * bound * noise[0].astype(f32)) / (2 * 4 * example_count)
+    return (final_output[None], factors[:, :example_count, 0])
+
+
 def solution(mesh):
     in_specs = (
         P("pipe", "tensor", "dp"),
@@ -93,4 +500,7 @@
         P("pipe", "tensor", "dp"),
     )
     out_specs = (P("pipe", "tensor", "dp"), P(None, "dp"))
-    return jax.shard_map(local, mesh=mesh, in_specs=in_specs, out_specs=out_specs, check_vma=False)
+    fits = mesh.shape["pipe"] == 2 and mesh.shape["dp"] == 4 and mesh.shape["tensor"] == 4
+    program = fast_local if fits else local
+    return jax.shard_map(
+        program, mesh=mesh, in_specs=in_specs, out_specs=out_specs, check_vma=False)

time: 418 us -> 154 us (0.37)
  waiting for transfers between devices: 233 us -> 0 us
  Pallas kernels: 0 us -> 133 us
  blocking collectives: 81.4 us -> 0 us
  matrix products: 41 us -> 16.1 us
  local copies, waits for them, and re-layouts: 23.4 us -> 3.1 us
  other arithmetic: 15.8 us -> 0 us
  between operations: 15.1 us -> 1.3 us
  starting transfers between devices: 7.54 us -> 0 us
    all_gather x4 -> x0, waiting for transfers between devices: 139 us -> none  [the longest x3 116 us: local(): incoming_gradient = lax.all_gather(current, 'tensor', axis=2, tiled=True)]
    pallas_call x0 -> x1, Pallas kernels: none -> 133 us  [fast_local(): pl.pallas_call(exchange_kernel, out_shape=(jax.ShapeDtypeStruct((2, 4, to...]
    reduce_scatter x2 -> x0, waiting for transfers between devices: 65.7 us -> none  [local(): lax.psum_scatter(lax.dot_general(scattered_rows, weight_block, (((1,), (1...]
    all_to_all x2 -> x0, blocking collectives: 57.8 us -> none  [local(): lax.all_to_all(by_block, 'dp', split_axis=1, concat_axis=0, tiled=True)]
    dot_general x7 -> x1, matrix products: 41 us -> 16.1 us  [fast_local(): lax.dot_general(clipped.reshape(-1, width), gradients.reshape(-1, column_...]
    psum x2 -> x0, blocking collectives: 23.6 us -> none  [the longest x1 20.9 us: local(): lax.psum(partial_grams.astype(jnp.bfloat16), 'tensor').astype(jnp.float32)]
    all_to_all x1 -> x0, waiting for transfers between devices: 23.3 us -> none  [local(): lax.all_to_all(by_block, 'dp', split_axis=1, concat_axis=0, tiled=True)]
    reshape x6 -> x0, local copies, waits for them, and re-layouts: 15.8 us -> none  [local(): by_block = incoming_gradient.reshape(token_count, group_count, column_part)]
  transfers between devices with their start and end apart: 9 -> 0, of which waited for: 9 -> 0; matrix products, arithmetic and copies ran while one was open for 6% -> 0% of each run, Pallas kernels for 0% -> 0%
where the time goes in v1:
time: 154 us
  Pallas kernels  133 us (86%)
  matrix products  16.1 us (10%)
  local copies, waits for them, and re-layouts  3.1 us (2%)
    pallas_call x1, Pallas kernels, fast_local(): pl.pallas_call(exchange_kernel, out_shape=(jax.ShapeDtypeStruct((2, 4, to...  133 us
    dot_general x1, matrix products, fast_local(): lax.dot_general(clipped.reshape(-1, width), gradients.reshape(-1, column_...  16.1 us

profile of v1, /device:TPU:0, one launch (start us, length us, event | category | flops | bytes accessed | tf_op | source)
XLA Modules:
  0.0 153.8 jit_solution(8111253375880972247)
XLA Ops:
  1.3 0.0 copy-start
  1.3 1.2 copy-done
  2.5 0.0 copy-start.1
  2.5 1.2 copy-done.1
  3.7 0.0 copy-start.2
  3.7 133.4 %exchange.1 = (bf16[2,4,128,2048]{3,2,1,0:T(8,128)(2,1)}, f32[2,8,128]{2,1,0:T(8,128)S(1)}, bf16[2,4,4,32,2048]{4,3,2,1,0:T(8,128)(2,1)}) custom-call(f32[1]{0:T(128)S(6)} %copy.7.bound_ref, bf16[2048,2048]{1,0:T(8,128)(2,1)} %bitcast.18, bf16[2,128,2048]{2,1,0:T(8,128)(2,1)S(1)} %bitcast.16, bf16[2,4,32,2048]{3,2,1,0:T(8,128)(2,1)S(1)} %bitcast.17), custom_call_target="tpu_custom_call" | custom-call | tf_op jit(solution)/shard_map/exchange/pallas_call | solution.py:445
  137.1 0.6 slice_reduce_fusion
  137.8 0.0 copy-done.2
  137.8 16.1 %fusion.1 = f32[1,2048,2048]{2,1,0:T(8,128)} fusion(bf16[1,2048,2048]{2,1,0:T(8,128)(2,1)S(1)} %copy-done.2, f32[]{:T(128)} %bitcast.5, bf16[1024,2048]{1,0:T(8,128)(2,1)} %bitcast.19, bf16[1024,2048]{1,0:T(8,128)(2,1)} %bitcast.20), kind=kOutput, calls=%fused_computation.2 | convolution fusion | flops 8606711808 | bytes 33554436 | tf_op jit(solution)/shard_map/dot_general | solution.py:484
Async XLA Ops:
  1.3 1.2 copy-start
  2.5 1.2 copy-start.1
  3.7 134.0 %copy-start.2 = (bf16[1,2048,2048]{2,1,0:T(8,128)(2,1)S(1)}, bf16[1,2048,2048]{2,1,0:T(8,128)(2,1)}, u32[]{:S(2)}) copy-start(bf16[1,2048,2048]{2,1,0:T(8,128)(2,1)} %param.9) | copy-start | bytes 25165828

commit v2 on v1

--- a/solution.py
+++ b/solution.py
@@ -199,10 +199,10 @@
         w_local.start()
 
     x_sends = [
-        remote(x_ref, xg.at[d], x_sem.at[0], x_recv.at[0], (p, xn, t)),
-        remote(x_ref, xg.at[d], x_sem.at[1], x_recv.at[1], (p, yn, t)),
+        remote(x_ref.at[m], xg.at[d, m], x_sem.at[2 * m + i], x_recv.at[2 * m + i], (p, near, t))
+        for m in range(2) for i, near in enumerate((xn, yn))
     ]
-    for copy in x_sends:
+    for copy in x_sends[:2]:
         copy.start()
 
     def gram(block):
@@ -226,16 +226,25 @@
     gin[p, t] = gin_send[p]
 
     def first_round(c, carry):
-        arrivals(zb1, 0, c, 1)
-        arrivals(zb1, 0, c, 2)
-
-        @pl.when(c < CHUNKS - 1)
-        def _():
-            own_send(zb1, 0, c + 1)
-            spread(0, c + 1, t)
-
-        arrivals(zb1, 0, c, 3)
-
+        @pl.when(c < CHUNKS)
+        def _():
+            arrivals(zb1, 0, c, 1)
+            arrivals(zb1, 0, c, 2)
+
+            @pl.when(c < CHUNKS - 1)
+            def _():
+                own_send(zb1, 0, c + 1)
+                spread(0, c + 1, t)
+
+            arrivals(zb1, 0, c, 3)
+
+        @pl.when(c > 0)
+        def _():
+            block_terms(c - 1)
+
+        return carry
+
+    def block_terms(c):
         @pl.when(c == 0)
         def _():
             @pl.when(p == 1)
@@ -271,7 +280,6 @@
         lax.fori_loop(0, width // 256, columns, 0)
         for step in (3, 1, 2):
             reduce_send(c, step).start()
-        return carry
 
     def reduce_send(c, step):
         target = lax.rem(d + step, 4)
@@ -280,7 +288,7 @@
             rs_send.at[c, step - 1], rs_recv.at[c, step - 1], (p, target, t),
         )
 
-    lax.fori_loop(0, CHUNKS, first_round, 0)
+    lax.fori_loop(0, CHUNKS + 1, first_round, 0)
 
     pair_remote = remote(g1c, g_ref.at[0], pair_send.at[0], pair_recv.at[0], (sibling, d, t))
     pair_local = pltpu.make_async_copy(g1c, g_ref.at[1], loc_sem.at[3])
@@ -304,14 +312,19 @@
         own_send(zb2, 1, c)
         spread(1, c, t)
 
-    remote(x_ref, xg.at[xn], x_sem.at[0], x_recv.at[0], (p, xn, t)).wait_recv()
-    remote(x_ref, xg.at[yn], x_sem.at[1], x_recv.at[1], (p, yn, t)).wait_recv()
+    def x_wait(m, i, slot, place):
+        index = 2 * m + i
+        remote(x_ref.at[m], xg.at[slot, m], x_sem.at[index], x_recv.at[index], (p, place, t)).wait_recv()
+
+    x_wait(0, 0, xn, xn)
+    x_wait(0, 1, yn, yn)
     forwards = [
-        remote(xg.at[xn, 0], xg.at[xn, 0], x_sem.at[2], x_recv.at[2], (p, yn, t)),
-        remote(xg.at[yn, 1], xg.at[yn, 1], x_sem.at[3], x_recv.at[3], (p, xn, t)),
+        remote(xg.at[xn, 0], xg.at[xn, 0], x_sem.at[4], x_recv.at[4], (p, yn, t)),
+        remote(xg.at[yn, 1], xg.at[yn, 1], x_sem.at[5], x_recv.at[5], (p, xn, t)),
     ]
-    for copy in forwards:
+    for copy in x_sends[2:]:
         copy.start()
+    forwards[0].start()
 
     make_own(0)
 
@@ -322,7 +335,11 @@
         arrivals(zb2, 1, c, 3)
         return carry
 
-    lax.fori_loop(0, CHUNKS - 1, second_round, 0)
+    lax.fori_loop(0, CHUNKS - 2, second_round, 0)
+    arrivals(zb2, 1, CHUNKS - 2, 1)
+    make_own(CHUNKS - 1)
+    x_wait(1, 1, yn, yn)
+    forwards[1].start()
 
     for copy in gram_sends:
         copy.wait_recv()
@@ -344,7 +361,8 @@
     ]
     for copy in norm_sends:
         copy.start()
-    arrivals(zb2, 1, CHUNKS - 1, 1)
+    arrivals(zb2, 1, CHUNKS - 2, 2)
+    arrivals(zb2, 1, CHUNKS - 2, 3)
     for copy in norm_sends:
         copy.wait_recv()
     bound = bound_ref[0]
@@ -359,13 +377,14 @@
                 factor_sends.append(remote(fb.at[p, d], fb.at[p, d], fs.at[index], fr.at[index], place))
     for copy in factor_sends:
         copy.start()
-    arrivals(zb2, 1, CHUNKS - 1, 2)
-    arrivals(zb2, 1, CHUNKS - 1, 3)
+    for distance in range(1, 4):
+        arrivals(zb2, 1, CHUNKS - 1, distance)
     for copy in factor_sends:
         copy.wait_recv()
     own[1].wait()
-    remote(xg.at[xn, 0], xg.at[diagonal, 0], x_sem.at[2], x_recv.at[2], (p, yn, t)).wait_recv()
-    remote(xg.at[yn, 1], xg.at[diagonal, 1], x_sem.at[3], x_recv.at[3], (p, xn, t)).wait_recv()
+    x_wait(1, 0, xn, xn)
+    remote(xg.at[xn, 0], xg.at[diagonal, 0], x_sem.at[4], x_recv.at[4], (p, yn, t)).wait_recv()
+    remote(xg.at[yn, 1], xg.at[diagonal, 1], x_sem.at[5], x_recv.at[5], (p, xn, t)).wait_recv()
 
     def scale(index, carry):
         j, m = index // 2, lax.rem(index, 2)
@@ -469,7 +488,7 @@
             vmem((2, 4, tokens, tokens), bf16),
             vmem((4, 8, 128), f32),
             vmem((2, 4, 8, 128), f32),
-            dma((1,)), dma((1,)), dma((4,)), dma((4,)), dma((4,)),
+            dma((1,)), dma((1,)), dma((6,)), dma((6,)), dma((4,)),
             dma((2, CHUNKS, 4, 2)), dma((2, CHUNKS, 4)),
             dma((CHUNKS, 4)), dma((CHUNKS, 4)), dma((CHUNKS, 4)), dma((2, 4, CHUNKS)),
             dma((CHUNKS, 3)), dma((CHUNKS, 3)),

time: 154 us -> 140 us (0.909)
  Pallas kernels: 133 us -> 119 us
    pallas_call x1, Pallas kernels: 133 us -> 119 us  [fast_local(): pl.pallas_call(exchange_kernel, out_shape=(jax.ShapeDtypeStruct((2, 4, to...]
where the time goes in v2:
time: 140 us
  Pallas kernels  119 us (85%)
  matrix products  16.1 us (12%)
  local copies, waits for them, and re-layouts  3.1 us (2%)
    pallas_call x1, Pallas kernels, fast_local(): pl.pallas_call(exchange_kernel, out_shape=(jax.ShapeDtypeStruct((2, 4, to...  119 us
    dot_general x1, matrix products, fast_local(): lax.dot_general(clipped.reshape(-1, width), gradients.reshape(-1, column_...  16.1 us

profile of v2, /device:TPU:0, one launch (start us, length us, event | category | flops | bytes accessed | tf_op | source)
XLA Modules:
  0.0 139.6 jit_solution(4970030415058216805)
XLA Ops:
  1.3 0.0 copy-start
  1.3 1.2 copy-done
  2.5 0.0 copy-start.1
  2.5 1.2 copy-done.1
  3.7 0.0 copy-start.2
  3.7 119.1 %exchange.1 = (bf16[2,4,128,2048]{3,2,1,0:T(8,128)(2,1)}, f32[2,8,128]{2,1,0:T(8,128)S(1)}, bf16[2,4,4,32,2048]{4,3,2,1,0:T(8,128)(2,1)}) custom-call(f32[1]{0:T(128)S(6)} %copy.7.bound_ref, bf16[2048,2048]{1,0:T(8,128)(2,1)} %bitcast.18, bf16[2,128,2048]{2,1,0:T(8,128)(2,1)S(1)} %bitcast.16, bf16[2,4,32,2048]{3,2,1,0:T(8,128)(2,1)S(1)} %bitcast.17), custom_call_target="tpu_custom_call" | custom-call | tf_op jit(solution)/shard_map/exchange/pallas_call | solution.py:464
  122.9 0.6 slice_reduce_fusion
  123.5 0.0 copy-done.2
  123.5 16.1 %fusion.1 = f32[1,2048,2048]{2,1,0:T(8,128)} fusion(bf16[1,2048,2048]{2,1,0:T(8,128)(2,1)S(1)} %copy-done.2, f32[]{:T(128)} %bitcast.5, bf16[1024,2048]{1,0:T(8,128)(2,1)} %bitcast.19, bf16[1024,2048]{1,0:T(8,128)(2,1)} %bitcast.20), kind=kOutput, calls=%fused_computation.2 | convolution fusion | flops 8606711808 | bytes 33554436 | tf_op jit(solution)/shard_map/dot_general | solution.py:503
Async XLA Ops:
  1.3 1.2 copy-start
  2.5 1.2 copy-start.1
  3.7 119.8 %copy-start.2 = (bf16[1,2048,2048]{2,1,0:T(8,128)(2,1)S(1)}, bf16[1,2048,2048]{2,1,0:T(8,128)(2,1)}, u32[]{:S(2)}) copy-start(bf16[1,2048,2048]{2,1,0:T(8,128)(2,1)} %param.9) | copy-start | bytes 25165828

commit v3 on v2

--- a/solution.py
+++ b/solution.py
@@ -226,17 +226,15 @@
     gin[p, t] = gin_send[p]
 
     def first_round(c, carry):
-        @pl.when(c < CHUNKS)
-        def _():
-            arrivals(zb1, 0, c, 1)
-            arrivals(zb1, 0, c, 2)
-
-            @pl.when(c < CHUNKS - 1)
-            def _():
-                own_send(zb1, 0, c + 1)
-                spread(0, c + 1, t)
-
-            arrivals(zb1, 0, c, 3)
+        arrivals(zb1, 0, c, 1)
+        arrivals(zb1, 0, c, 2)
+
+        @pl.when(c < CHUNKS - 1)
+        def _():
+            own_send(zb1, 0, c + 1)
+            spread(0, c + 1, t)
+
+        arrivals(zb1, 0, c, 3)
 
         @pl.when(c > 0)
         def _():
@@ -288,18 +286,6 @@
             rs_send.at[c, step - 1], rs_recv.at[c, step - 1], (p, target, t),
         )
 
-    lax.fori_loop(0, CHUNKS + 1, first_round, 0)
-
-    pair_remote = remote(g1c, g_ref.at[0], pair_send.at[0], pair_recv.at[0], (sibling, d, t))
-    pair_local = pltpu.make_async_copy(g1c, g_ref.at[1], loc_sem.at[3])
-
-    @pl.when(p == 0)
-    def _():
-        pair_remote.start()
-
-    @pl.when(p == 1)
-    def _():
-        pair_local.start()
 
     def make_own(c):
         for step in range(1, 4):
@@ -312,6 +298,21 @@
         own_send(zb2, 1, c)
         spread(1, c, t)
 
+    lax.fori_loop(0, CHUNKS, first_round, 0)
+    make_own(0)
+    block_terms(CHUNKS - 1)
+
+    pair_remote = remote(g1c, g_ref.at[0], pair_send.at[0], pair_recv.at[0], (sibling, d, t))
+    pair_local = pltpu.make_async_copy(g1c, g_ref.at[1], loc_sem.at[3])
+
+    @pl.when(p == 0)
+    def _():
+        pair_remote.start()
+
+    @pl.when(p == 1)
+    def _():
+        pair_local.start()
+
     def x_wait(m, i, slot, place):
         index = 2 * m + i
         remote(x_ref.at[m], xg.at[slot, m], x_sem.at[index], x_recv.at[index], (p, place, t)).wait_recv()
@@ -326,7 +327,6 @@
         copy.start()
     forwards[0].start()
 
-    make_own(0)
 
     def second_round(c, carry):
         arrivals(zb2, 1, c, 1)

time: 140 us -> 139 us (level)
  no operation moved by 1% of the time
where the time goes in v3:
time: 139 us
  Pallas kernels  119 us (86%)
  matrix products  16.1 us (12%)
  local copies, waits for them, and re-layouts  3.1 us (2%)
    pallas_call x1, Pallas kernels, fast_local(): pl.pallas_call(exchange_kernel, out_shape=(jax.ShapeDtypeStruct((2, 4, to...  119 us
    dot_general x1, matrix products, fast_local(): lax.dot_general(clipped.reshape(-1, width), gradients.reshape(-1, column_...  16.1 us

profile of v3, /device:TPU:0, one launch (start us, length us, event | category | flops | bytes accessed | tf_op | source)
XLA Modules:
  0.0 139.3 jit_solution(1544971887700734873)
XLA Ops:
  1.3 0.0 copy-start
  1.3 1.2 copy-done
  2.5 0.0 copy-start.1
  2.5 1.2 copy-done.1
  3.7 0.0 copy-start.2
  3.7 118.8 %exchange.1 = (bf16[2,4,128,2048]{3,2,1,0:T(8,128)(2,1)}, f32[2,8,128]{2,1,0:T(8,128)S(1)}, bf16[2,4,4,32,2048]{4,3,2,1,0:T(8,128)(2,1)}) custom-call(f32[1]{0:T(128)S(6)} %copy.7.bound_ref, bf16[2048,2048]{1,0:T(8,128)(2,1)} %bitcast.18, bf16[2,128,2048]{2,1,0:T(8,128)(2,1)S(1)} %bitcast.16, bf16[2,4,32,2048]{3,2,1,0:T(8,128)(2,1)S(1)} %bitcast.17), custom_call_target="tpu_custom_call" | custom-call | tf_op jit(solution)/shard_map/exchange/pallas_call | solution.py:464
  122.6 0.6 slice_reduce_fusion
  123.2 0.0 copy-done.2
  123.2 16.1 %fusion.1 = f32[1,2048,2048]{2,1,0:T(8,128)} fusion(bf16[1,2048,2048]{2,1,0:T(8,128)(2,1)S(1)} %copy-done.2, f32[]{:T(128)} %bitcast.5, bf16[1024,2048]{1,0:T(8,128)(2,1)} %bitcast.19, bf16[1024,2048]{1,0:T(8,128)(2,1)} %bitcast.20), kind=kOutput, calls=%fused_computation.2 | convolution fusion | flops 8606711808 | bytes 33554436 | tf_op jit(solution)/shard_map/dot_general | solution.py:503
Async XLA Ops:
  1.3 1.2 copy-start
  2.5 1.2 copy-start.1
  3.7 119.5 %copy-start.2 = (bf16[1,2048,2048]{2,1,0:T(8,128)(2,1)S(1)}, bf16[1,2048,2048]{2,1,0:T(8,128)(2,1)}, u32[]{:S(2)}) copy-start(bf16[1,2048,2048]{2,1,0:T(8,128)(2,1)} %param.9) | copy-start | bytes 25165828
